TPU v7x, 256 devices: a whole 4x4x8 slice. The times are simulated.
256 devices in a mesh: dp: 2 (over core), seq: 16 (over z, y_hi), chan: 8 (over y_lo, x).
Axes of the slice: x: 4, y: 4 (y_hi: 2, y_lo: 2; y = y_hi * 2 + y_lo), z: 8, core: 2. Of those that a mesh axis runs over, the one named last changes fastest.
Arguments:
- features: bfloat16 [4096, 3, 8192], P(('dp', 'seq'), None, 'chan'), parts along dimension 0, may hold values from -6 to 6
- lengths: int32 [6], P('dp'), parts along dimension 0, may hold values from 1 to 1024, 2048 in all
- ids: int32 [4096], P(('dp', 'seq')), parts along dimension 0, may hold values from 0 to 511
- taps: float32 [3, 3, 8192], P(None, None, 'chan'), may hold values from -3.5 to 3.5
- filters: float32 [8192, 2048], P(('chan', 'seq')), as said below
- skip: float32 [8192], P(('chan', 'seq')), may hold values from 0.5 to 1.5
- out_weight: bfloat16 [8192, 8192], P('chan', 'seq'), may hold values from -0.0625 to 0.0625
- embedding: bfloat16 [512, 8192], P(None, 'chan'), may hold values from -6 to 6
Outputs:
- mixed: bfloat16 [4096, 8192], P(('dp', 'seq'), 'chan'), parts along dimension 0
There are 2 independent parts, one for each index of `dp`. A program takes and returns all parts, laid end to end along the dimension named above; an argument that names none is the same for every part. Nothing has to cross between parts.
Inputs may be any that keep to these rules, and one draw needn't show every extreme that they name: `lengths`: the 3 documents fill the segment one after another and sum to 2048; the longest holds exactly 1024 positions. `filters`: positive.
All inputs are finite; a program needn't handle non-finite values.
Results may differ from a plain program's by a relative error of at most 0.022.
Values may be sent and summed in bfloat16 or wider, within the bound.
A program may use at most 128 MiB of HBM per device.

v0:
```python
import jax
import jax.numpy as jnp
from jax import lax
from jax.experimental import pallas as pl
from jax.experimental.pallas import tpu as pltpu
from jax.sharding import PartitionSpec as P

MESH = pl.DeviceIdType.MESH
F32, BF16 = jnp.float32, jnp.bfloat16
B = 128
SEQ, CHAN, Z = 16, 8, 8
OWN = 64
LAGS = 8
PITCH = 65


def build_toeplitz(filt_ref, toep_ref, first, last):
    row = lax.broadcasted_iota(jnp.int32, (B, B), 0)
    col = lax.broadcasted_iota(jnp.int32, (B, B), 1)
    upper = col >= row

    def step(g, _):
        taps = filt_ref[pl.ds(pl.multiple_of(g * 8, 8), 8), :]
        for j in range(8):
            before = jnp.zeros((B, B), F32)
            for d in range(LAGS + 1):
                if d < LAGS:
                    line = jnp.broadcast_to(taps[j : j + 1, d * B : (d + 1) * B], (B, B))
                    now = pltpu.roll(line, 0, 1, stride=1, stride_axis=0)
                else:
                    now = jnp.zeros((B, B), F32)
                toep_ref[g * 8 + j, d * B : (d + 1) * B, :] = jnp.where(upper, now, before).astype(BF16)
                before = now
        return 0

    lax.fori_loop(first, last, step, 0)


def document(position, b1, b2):
    return (position >= b1).astype(jnp.int32) + (position >= b2).astype(jnp.int32)


def short_convolve(feat_ref, taps_ref, halo_ref, cols_ref, s, b1, b2):
    row = lax.broadcasted_iota(jnp.int32, (B, B), 0)
    position = s * B + row
    here = document(position, b1, b2)
    agree1 = ((document(position - 1, b1, b2) == here) & (position >= 1)).astype(F32)
    agree2 = ((document(position - 2, b1, b2) == here) & (position >= 2)).astype(F32)
    for n in range(8):
        cols = slice(n * B, (n + 1) * B)
        halo = halo_ref[:, cols].astype(F32)
        short = []
        for g in range(3):
            x = feat_ref[g, :, cols].astype(F32)
            older, newer = halo[2 * g : 2 * g + 1], halo[2 * g + 1 : 2 * g + 2]
            x1 = jnp.where(row < 1, newer, pltpu.roll(x, 1, 0))
            x2 = jnp.where(row < 1, older, jnp.where(row < 2, newer, pltpu.roll(x, 2, 0)))
            t = taps_ref[:, g, cols]
            running = t[0:1] * x + t[1:2] * x1 * agree1 + t[2:3] * x2 * agree2
            short.append(running.astype(BF16))
        product = (short[1].astype(F32) * short[2].astype(F32)).astype(BF16).T
        query = short[0].T
        for h in range(2):
            cols_ref[2 * n + h, 0:OWN, :] = product[h * OWN : (h + 1) * OWN]
            cols_ref[2 * n + h, OWN:B, :] = query[h * OWN : (h + 1) * OWN]


def long_convolve(toep_ref, x_ref, y_ref, b1, b2):
    block = lax.broadcasted_iota(jnp.int32, (SEQ, B), 0)
    lane = lax.broadcasted_iota(jnp.int32, (SEQ, B), 1)

    def docs(d):
        return document((block - d) * B + lane, b1, b2)

    masks = [[(docs(d) == k).astype(F32).astype(BF16) for d in range(LAGS + 1)] for k in range(3)]
    here = docs(0)

    def step(c, _):
        lhs = []
        for d in range(LAGS + 1):
            x = x_ref[pl.ds((LAGS - d) * PITCH + c, SEQ, stride=PITCH), :].astype(BF16)
            lhs.append(jnp.concatenate([masks[k][d] * x for k in range(3)], axis=0))
        y = jnp.dot(jnp.concatenate(lhs, axis=1), toep_ref[c], preferred_element_type=F32)
        y_ref[pl.ds(c, SEQ, stride=PITCH), :] = jnp.where(
            here == 0, y[0:SEQ], jnp.where(here == 1, y[SEQ : 2 * SEQ], y[2 * SEQ : 3 * SEQ])
        )
        return 0

    lax.fori_loop(0, OWN, step, 0, unroll=8)


def kernel(
    len_ref, feat_ref, taps_ref, filt_ref, skip_ref, w_ref, ids_ref, emb_ref, out_ref,
    halo_out, halo_in, cols_ref, rows_ref, toep_ref, x_ref, y_ref, gated_ref, wt_ref, g_ref,
    part_ref, got_ref, sum_ref, plane_ref, last_ref, look_ref,
    halo_s, halo_r, w_s, w_r, a_s, a_r, y_s, y_r, up_s, up_r, down_s, down_r, rs_s, rs_r, z_s, z_r, f_s, f_r,
):
    dp = lax.axis_index("dp")
    s = lax.axis_index("seq")
    k = lax.axis_index("chan")
    z, half = s // 2, s % 2
    b1 = len_ref[0]
    b2 = b1 + len_ref[1]

    def remote(src, dst, send, recv, seq, chan):
        return pltpu.make_async_remote_copy(
            src_ref=src, dst_ref=dst, send_sem=send, recv_sem=recv, device_id=(dp, seq, chan), device_id_type=MESH
        )

    barrier = pltpu.get_barrier_semaphore()
    for d in range(1, SEQ):
        pl.semaphore_signal(barrier, inc=1, device_id=(dp, (s + d) % SEQ, k), device_id_type=MESH)
    for d in range(1, CHAN):
        pl.semaphore_signal(barrier, inc=1, device_id=(dp, s, (k + d) % CHAN), device_id_type=MESH)

    for a in range(8):
        for b in range(4):
            wt_ref[half * 4 + b, :, a * B : (a + 1) * B] = w_ref[a * B : (a + 1) * B, b * B : (b + 1) * B].T
    edge = [feat_ref[g, B - 16 : B, :].astype(F32)[14:16] for g in range(3)]
    halo_out[...] = jnp.concatenate(edge + [jnp.zeros((10, CHAN * B), F32)], axis=0).astype(BF16)
    pl.semaphore_wait(barrier, SEQ - 1 + CHAN - 1)

    halo_copy = remote(halo_out, halo_in, halo_s, halo_r, (s + 1) % SEQ, k)
    halo_copy.start()
    mine = wt_ref.at[pl.ds(half * 4, 4)]
    w_copy = remote(mine, mine, w_s, w_r, z * 2 + 1 - half, k)
    w_copy.start()
    build_toeplitz(filt_ref, toep_ref, 0, 2)
    halo_copy.wait()
    short_convolve(feat_ref, taps_ref, halo_in, cols_ref, s, b1, b2)

    spread = []
    for d in range(1, SEQ):
        to = (s + d) % SEQ
        copy = remote(cols_ref.at[to], rows_ref.at[s], a_s.at[d], a_r.at[d], to, k)
        copy.start()
        spread.append(copy)
    rows_ref[s] = cols_ref[s]
    build_toeplitz(filt_ref, toep_ref, 2, 8)

    wanted = jnp.broadcast_to(ids_ref[...], (B, B)).T
    lane = lax.broadcasted_iota(jnp.int32, (B, B), 1)
    vocab = emb_ref.shape[0] // B
    hot = jnp.concatenate([(wanted == lane + v * B).astype(F32).astype(BF16) for v in range(vocab)], axis=1)
    for n in range(8):
        cols = slice(n * B, (n + 1) * B)
        look_ref[:, cols] = jnp.dot(hot, emb_ref[:, cols], preferred_element_type=F32).astype(BF16)
    skip = jnp.broadcast_to(skip_ref[...], (B, OWN)).T

    for copy in spread:
        copy.wait()
    x_ref[0 : LAGS * PITCH, :] = jnp.zeros((LAGS * PITCH, B), F32)
    for i in range(SEQ):
        at = (LAGS + i) * PITCH
        x_ref[at : at + OWN, :] = rows_ref[i, 0:OWN, :].astype(F32)
    long_convolve(toep_ref, x_ref, y_ref, b1, b2)
    for i in range(SEQ):
        signal = rows_ref[i, 0:OWN, :].astype(F32)
        convolved = (y_ref[i * PITCH : i * PITCH + OWN, :] + skip * signal).astype(BF16)
        gated = rows_ref[i, OWN:B, :].astype(F32) * convolved.astype(F32)
        place = i // 2 // 2 + 4 * (i // 2 % 2)
        gated_ref[i % 2, place] = gated.astype(BF16)

    mate = []
    for j in range(4):
        copy = remote(
            gated_ref.at[1 - half, pl.ds(2 * j, 2)], g_ref.at[pl.ds(2 * j, 2), z, half], y_s.at[j], y_r.at[j],
            z * 2 + 1 - half, k,
        )
        copy.start()
        mate.append(copy)
    for q in range(8):
        g_ref[q, z, half] = gated_ref[half, q]

    up_seq, down_seq = (z + 1) % Z * 2 + half, (z + Z - 1) % Z * 2 + half

    def up(j, n):
        block = g_ref.at[pl.ds(2 * j, 2), (z + Z - n + 1) % Z]
        return remote(block, block, up_s.at[j, n], up_r.at[j, n], up_seq, k)

    def down(j, n):
        block = g_ref.at[pl.ds(2 * j, 2), (z + n - 1) % Z]
        return remote(block, block, down_s.at[j, n], down_r.at[j, n], down_seq, k)

    def up_has(j, n):
        return n <= 3 + (j % 2 == 0)

    def down_has(j, n):
        return n <= 3 + (j % 2 == 1)

    def own(j):
        mate[j].wait_recv()
        up(j, 1).start()
        down(j, 1).start()

    def forward(j, n):
        if up_has(j, n):
            up(j, n).wait_recv()
            if up_has(j, n + 1):
                up(j, n + 1).start()
        if down_has(j, n):
            down(j, n).wait_recv()
            if down_has(j, n + 1):
                down(j, n + 1).start()

    sent = []

    def project(t):
        rhs = jnp.concatenate([g_ref[4 * t + q].reshape(Z * B, B) for q in range(4)], axis=1)
        for d in [1, 7, 2, 6, 3, 5, 4, 0]:
            to = (k + d) % CHAN
            value = jnp.dot(wt_ref[to], rhs, preferred_element_type=F32).astype(BF16)
            for q in range(4):
                part_ref[t, d, q] = value[:, q * B : (q + 1) * B]
            if d:
                copy = remote(part_ref.at[t, d], got_ref.at[t, d], rs_s.at[t, d], rs_r.at[t, d], s, to)
                copy.start()
                sent.append((t, copy))

    def collect(t):
        for u, copy in sent:
            if u == t:
                copy.wait_recv()
        for q in range(4):
            total = part_ref[t, 0, q].astype(F32)
            for d in range(1, CHAN):
                total = total + got_ref[t, d, q].astype(F32)
            sum_ref[t, q] = total.T.astype(BF16)
        for q in range(4):
            to = 2 * q + t

            @pl.when(z != to)
            def _():
                remote(sum_ref.at[t, q], plane_ref.at[z], z_s.at[t, q], z_r.at[z], to * 2 + half, k).start()

            @pl.when(z == to)
            def _():
                plane_ref[to] = sum_ref[t, q]

    own(0)
    own(1)
    for n in (1, 2, 3):
        forward(0, n)
        forward(1, n)
    own(2)
    own(3)
    forward(0, 4)
    forward(1, 4)
    w_copy.wait()
    project(0)
    for n in (1, 2, 3, 4):
        forward(2, n)
        forward(3, n)
    project(1)
    collect(0)
    collect(1)

    for zz in range(Z):

        @pl.when(z != zz)
        def _():
            remote(sum_ref.at[0, 0], plane_ref.at[zz], z_s.at[0, 0], z_r.at[zz], zz * 2 + half, k).wait_recv()

        @pl.when(k != zz)
        def _():
            remote(plane_ref.at[zz], last_ref.at[k], f_s.at[zz], f_r.at[k], s, zz).start()

        @pl.when(k == zz)
        def _():
            last_ref[zz] = plane_ref[zz]

    for kk in range(CHAN):

        @pl.when(k != kk)
        def _():
            remote(plane_ref.at[0], last_ref.at[kk], f_s.at[0], f_r.at[kk], s, kk).wait_recv()

        cols = slice(kk * B, (kk + 1) * B)
        out_ref[:, cols] = (last_ref[kk].astype(F32) + look_ref[:, cols].astype(F32)).astype(BF16)

    for copy in mate:
        copy.wait_send()
    for j in range(4):
        for n in range(1, 5):
            if up_has(j, n):
                up(j, n).wait_send()
            if down_has(j, n):
                down(j, n).wait_send()
    for _, copy in sent:
        copy.wait_send()
    for t in range(2):
        for q in range(4):

            @pl.when(z != 2 * q + t)
            def _():
                remote(sum_ref.at[t, q], plane_ref.at[z], z_s.at[t, q], z_r.at[z], 2 * (2 * q + t) + half, k).wait_send()

    for zz in range(Z):

        @pl.when(k != zz)
        def _():
            remote(plane_ref.at[zz], last_ref.at[k], f_s.at[zz], f_r.at[k], s, zz).wait_send()


def local(features, lengths, ids, taps, filters, skip, out_weight, embedding):
    vmem = pl.BlockSpec(memory_space=pltpu.VMEM)
    dma = pltpu.SemaphoreType.DMA
    tile = (B, B)
    return pl.pallas_call(
        kernel,
        out_shape=jax.ShapeDtypeStruct((B, CHAN * B), BF16),
        in_specs=[pl.BlockSpec(memory_space=pltpu.SMEM)] + [vmem] * 7,
        out_specs=vmem,
        scratch_shapes=[
            pltpu.VMEM((16, CHAN * B), BF16),
            pltpu.VMEM((16, CHAN * B), BF16),
            pltpu.VMEM((SEQ,) + tile, BF16),
            pltpu.VMEM((SEQ,) + tile, BF16),
            pltpu.VMEM((OWN, (LAGS + 1) * B, B), BF16),
            pltpu.VMEM(((LAGS + SEQ) * PITCH, B), F32),
            pltpu.VMEM((SEQ * PITCH, B), F32),
            pltpu.VMEM((2, 8, OWN, B), BF16),
            pltpu.VMEM((8, B, CHAN * B), BF16),
            pltpu.VMEM((8, Z, 2, OWN, B), BF16),
            pltpu.VMEM((2, CHAN, 4) + tile, BF16),
            pltpu.VMEM((2, CHAN, 4) + tile, BF16),
            pltpu.VMEM((2, 4) + tile, BF16),
            pltpu.VMEM((Z,) + tile, BF16),
            pltpu.VMEM((CHAN,) + tile, BF16),
            pltpu.VMEM((B, CHAN * B), BF16),
            dma, dma, dma, dma,
            dma((SEQ,)), dma((SEQ,)),
            dma((4,)), dma((4,)),
            dma((4, 5)), dma((4, 5)), dma((4, 5)), dma((4, 5)),
            dma((2, CHAN)), dma((2, CHAN)),
            dma((2, 4)), dma((Z,)),
            dma((Z,)), dma((CHAN,)),
        ],
        compiler_params=pltpu.CompilerParams(
            collective_id=0, has_side_effects=True, vmem_limit_bytes=56 * 2**20
        ),
        name="hyena_block",
    )(
        lengths,
        features.transpose(1, 0, 2),
        taps,
        filters,
        skip.reshape(1, -1),
        out_weight,
        ids.reshape(1, -1),
        embedding,
    )


def solution(mesh):
    placed = (
        P(("dp", "seq"), None, "chan"),
        P("dp"),
        P(("dp", "seq")),
        P(None, None, "chan"),
        P(("chan", "seq"), None),
        P(("chan", "seq")),
        P("chan", "seq"),
        P(None, "chan"),
    )
    return jax.shard_map(
        local, mesh=mesh, in_specs=placed, out_specs=P(("dp", "seq"), "chan"), check_vma=False
    )
```

profile of v0, /device:TPU:104, one launch (start us, length us, event | category | flops | bytes accessed | tf_op | source)
XLA Modules:
  0.0 105.0 jit_solution(14890349088562822749)
XLA Ops:
  0.0 103.3 %hyena_block.1 = bf16[128,1024]{1,0:T(8,128)(2,1)} custom-call(s32[3]{0:T(128)} %len_ref.1, bf16[3,128,1024]{2,1,0:T(8,128)(2,1)} %bitcast.3, f32[3,3,1024]{2,1,0:T(4,128)} %taps_ref.1, f32[64,2048]{1,0:T(8,128)} %filt_ref.1, f32[1,64]{1,0:T(1,128)} %bitcast.4, bf16[1024,512]{1,0:T(8,128)(2,1)} %w_ref.1, s32[1,128]{1,0:T(1,128)} %bitcast.5, ...), custom_call_target="tpu_custom_call" | custom-call | tf_op jit(solution)/shard_map/hyena_block/pallas_call | solution.py:309
  103.3 1.7 %copy.10 = bf16[128,1024]{1,0:T(8,128)(2,1)} copy(bf16[128,1024]{1,0:T(8,128)(2,1)} %hyena_block.1) | data formatting | bytes 524288
where the time goes:
time: 107 us; the launch traced here: 105 us
  Pallas kernels  103 us (96%)
  local copies, waits for them, and re-layouts  1.67 us (2%)
    pallas_call x1, Pallas kernels, local(): pl.pallas_call(kernel, out_shape=jax.ShapeDtypeStruct((B, CHAN * B), BF16...  103 us

commit v1 on v0

--- a/solution.py
+++ b/solution.py
@@ -90,54 +90,62 @@
 
 
 def kernel(
-    len_ref, feat_ref, taps_ref, filt_ref, skip_ref, w_ref, ids_ref, emb_ref, out_ref,
-    halo_out, halo_in, cols_ref, rows_ref, toep_ref, x_ref, y_ref, gated_ref, wt_ref, g_ref,
+    len_ref, feat_ref, taps_ref, filt_ref, skip_ref, w_hbm, ids_ref, emb_hbm, out_ref,
+    halo_out, halo_in, cols_ref, rows_ref, toep_ref, x_ref, y_ref, gated_ref, pair_ref, w_ref, emb_ref, g_ref,
     part_ref, got_ref, sum_ref, plane_ref, last_ref, look_ref,
-    halo_s, halo_r, w_s, w_r, a_s, a_r, y_s, y_r, up_s, up_r, down_s, down_r, rs_s, rs_r, z_s, z_r, f_s, f_r,
+    own_s, emb_s, halo_s, halo_r, w_s, w_r, sib_s, sib_r, p_s, p_r, q_s, q_r, y_s, y_r,
+    up_s, up_r, down_s, down_r, rs_s, rs_r, z_s, z_r, f_s, f_r,
 ):
     dp = lax.axis_index("dp")
     s = lax.axis_index("seq")
     k = lax.axis_index("chan")
     z, half = s // 2, s % 2
-    b1 = len_ref[0]
-    b2 = b1 + len_ref[1]
-
-    def remote(src, dst, send, recv, seq, chan):
-        return pltpu.make_async_remote_copy(
-            src_ref=src, dst_ref=dst, send_sem=send, recv_sem=recv, device_id=(dp, seq, chan), device_id_type=MESH
-        )
+    mate_seq = z * 2 + 1 - half
 
     barrier = pltpu.get_barrier_semaphore()
     for d in range(1, SEQ):
         pl.semaphore_signal(barrier, inc=1, device_id=(dp, (s + d) % SEQ, k), device_id_type=MESH)
     for d in range(1, CHAN):
         pl.semaphore_signal(barrier, inc=1, device_id=(dp, s, (k + d) % CHAN), device_id_type=MESH)
-
-    for a in range(8):
-        for b in range(4):
-            wt_ref[half * 4 + b, :, a * B : (a + 1) * B] = w_ref[a * B : (a + 1) * B, b * B : (b + 1) * B].T
+    pl.semaphore_signal(barrier, inc=1, device_id=(1 - dp, s, k), device_id_type=MESH)
+
+    own_w = [
+        pltpu.make_async_copy(w_hbm.at[:, pl.ds(b * B, B)], w_ref.at[half * 4 + b], own_s.at[b]) for b in range(4)
+    ]
+    emb_copy = pltpu.make_async_copy(emb_hbm, emb_ref, emb_s)
+    for copy in own_w:
+        copy.start()
+    emb_copy.start()
+
+    b1 = len_ref[0]
+    b2 = b1 + len_ref[1]
+
+    def remote(src, dst, send, recv, seq, chan, core=dp):
+        return pltpu.make_async_remote_copy(
+            src_ref=src, dst_ref=dst, send_sem=send, recv_sem=recv, device_id=(core, seq, chan), device_id_type=MESH
+        )
+
     edge = [feat_ref[g, B - 16 : B, :].astype(F32)[14:16] for g in range(3)]
     halo_out[...] = jnp.concatenate(edge + [jnp.zeros((10, CHAN * B), F32)], axis=0).astype(BF16)
-    pl.semaphore_wait(barrier, SEQ - 1 + CHAN - 1)
+    pl.semaphore_wait(barrier, SEQ - 1 + CHAN - 1 + 1)
 
     halo_copy = remote(halo_out, halo_in, halo_s, halo_r, (s + 1) % SEQ, k)
     halo_copy.start()
-    mine = wt_ref.at[pl.ds(half * 4, 4)]
-    w_copy = remote(mine, mine, w_s, w_r, z * 2 + 1 - half, k)
-    w_copy.start()
     build_toeplitz(filt_ref, toep_ref, 0, 2)
     halo_copy.wait()
     short_convolve(feat_ref, taps_ref, halo_in, cols_ref, s, b1, b2)
 
     spread = []
-    for d in range(1, SEQ):
-        to = (s + d) % SEQ
-        copy = remote(cols_ref.at[to], rows_ref.at[s], a_s.at[d], a_r.at[d], to, k)
-        copy.start()
-        spread.append(copy)
+    for rows, send, recv in ((pl.ds(0, OWN), p_s, p_r), (pl.ds(OWN, OWN), q_s, q_r)):
+        for d in range(1, SEQ):
+            to = (s + d) % SEQ
+            copy = remote(cols_ref.at[to, rows], rows_ref.at[s, rows], send.at[d], recv.at[d], to, k)
+            copy.start()
+            spread.append(copy)
     rows_ref[s] = cols_ref[s]
     build_toeplitz(filt_ref, toep_ref, 2, 8)
 
+    emb_copy.wait()
     wanted = jnp.broadcast_to(ids_ref[...], (B, B)).T
     lane = lax.broadcasted_iota(jnp.int32, (B, B), 1)
     vocab = emb_ref.shape[0] // B
@@ -147,30 +155,38 @@
         look_ref[:, cols] = jnp.dot(hot, emb_ref[:, cols], preferred_element_type=F32).astype(BF16)
     skip = jnp.broadcast_to(skip_ref[...], (B, OWN)).T
 
-    for copy in spread:
+    for copy in spread[: SEQ - 1]:
         copy.wait()
     x_ref[0 : LAGS * PITCH, :] = jnp.zeros((LAGS * PITCH, B), F32)
     for i in range(SEQ):
         at = (LAGS + i) * PITCH
         x_ref[at : at + OWN, :] = rows_ref[i, 0:OWN, :].astype(F32)
     long_convolve(toep_ref, x_ref, y_ref, b1, b2)
+    for copy in spread[SEQ - 1 :]:
+        copy.wait()
     for i in range(SEQ):
         signal = rows_ref[i, 0:OWN, :].astype(F32)
         convolved = (y_ref[i * PITCH : i * PITCH + OWN, :] + skip * signal).astype(BF16)
         gated = rows_ref[i, OWN:B, :].astype(F32) * convolved.astype(F32)
-        place = i // 2 // 2 + 4 * (i // 2 % 2)
-        gated_ref[i % 2, place] = gated.astype(BF16)
+        owner = i // 2
+        gated_ref[i % 2, 2 * (owner % 4) + owner // 4] = gated.astype(BF16)
 
     mate = []
     for j in range(4):
-        copy = remote(
-            gated_ref.at[1 - half, pl.ds(2 * j, 2)], g_ref.at[pl.ds(2 * j, 2), z, half], y_s.at[j], y_r.at[j],
-            z * 2 + 1 - half, k,
-        )
+        two = pl.ds(2 * j, 2)
+        copy = remote(gated_ref.at[1 - half, two], pair_ref.at[two, half], y_s.at[j], y_r.at[j], mate_seq, k)
         copy.start()
         mate.append(copy)
+    for copy in own_w:
+        copy.wait()
+    depth = w_ref.shape[1] // 2
+    mine = w_ref.at[pl.ds(half * 4, 4), pl.ds(dp * depth, depth)]
+    w_copy = remote(mine, mine, w_s, w_r, mate_seq, k)
+    w_copy.start()
+    theirs = w_ref.at[pl.ds((1 - half) * 4, 4), pl.ds(dp * depth, depth)]
+    w_share = remote(theirs, theirs, sib_s, sib_r, s, k, 1 - dp)
     for q in range(8):
-        g_ref[q, z, half] = gated_ref[half, q]
+        pair_ref[q, half] = gated_ref[half, q]
 
     up_seq, down_seq = (z + 1) % Z * 2 + half, (z + Z - 1) % Z * 2 + half
 
@@ -190,6 +206,8 @@
 
     def own(j):
         mate[j].wait_recv()
+        for q in (2 * j, 2 * j + 1):
+            g_ref[q, z] = pair_ref[q].reshape(B, B).T
         up(j, 1).start()
         down(j, 1).start()
 
@@ -205,55 +223,75 @@
 
     sent = []
 
-    def project(t):
-        rhs = jnp.concatenate([g_ref[4 * t + q].reshape(Z * B, B) for q in range(4)], axis=1)
-        for d in [1, 7, 2, 6, 3, 5, 4, 0]:
-            to = (k + d) % CHAN
-            value = jnp.dot(wt_ref[to], rhs, preferred_element_type=F32).astype(BF16)
-            for q in range(4):
-                part_ref[t, d, q] = value[:, q * B : (q + 1) * B]
-            if d:
-                copy = remote(part_ref.at[t, d], got_ref.at[t, d], rs_s.at[t, d], rs_r.at[t, d], s, to)
+    def project(j):
+        lhs = jnp.concatenate(
+            [jnp.concatenate([g_ref[q, zz] for zz in range(Z)], axis=1) for q in (2 * j, 2 * j + 1)], axis=0
+        )
+        for pair in ((1, 7), (2, 6), (3, 5), (4, 0)):
+            rhs = jnp.concatenate([w_ref[(k + d) % CHAN] for d in pair], axis=1)
+            value = jnp.dot(lhs, rhs, preferred_element_type=F32).astype(BF16)
+            for n, d in enumerate(pair):
+                for q in range(2):
+                    part_ref[j, d, q] = value[q * B : (q + 1) * B, n * B : (n + 1) * B]
+                if d:
+                    copy = remote(
+                        part_ref.at[j, d], got_ref.at[j, d], rs_s.at[j, d], rs_r.at[j, d], s, (k + d) % CHAN
+                    )
+                    copy.start()
+                    sent.append((j, copy))
+
+    def to_plane(j, q):
+        owner = j + 4 * q
+        return owner, remote(sum_ref.at[j, q], plane_ref.at[z], z_s.at[j, q], z_r.at[z], owner * 2 + half, k)
+
+    def collect(j):
+        for u, copy in sent:
+            if u == j:
+                copy.wait_recv()
+        for q in range(2):
+            total = part_ref[j, 0, q].astype(F32)
+            for d in range(1, CHAN):
+                total = total + got_ref[j, d, q].astype(F32)
+            sum_ref[j, q] = total.astype(BF16)
+            owner, copy = to_plane(j, q)
+
+            @pl.when(z != owner)
+            def _():
                 copy.start()
-                sent.append((t, copy))
-
-    def collect(t):
-        for u, copy in sent:
-            if u == t:
-                copy.wait_recv()
-        for q in range(4):
-            total = part_ref[t, 0, q].astype(F32)
-            for d in range(1, CHAN):
-                total = total + got_ref[t, d, q].astype(F32)
-            sum_ref[t, q] = total.T.astype(BF16)
-        for q in range(4):
-            to = 2 * q + t
-
-            @pl.when(z != to)
+
+            @pl.when(z == owner)
             def _():
-                remote(sum_ref.at[t, q], plane_ref.at[z], z_s.at[t, q], z_r.at[z], to * 2 + half, k).start()
-
-            @pl.when(z == to)
-            def _():
-                plane_ref[to] = sum_ref[t, q]
+                plane_ref[owner] = sum_ref[j, q]
 
     own(0)
     own(1)
-    for n in (1, 2, 3):
-        forward(0, n)
-        forward(1, n)
+    forward(0, 1)
     own(2)
+    forward(1, 1)
+    forward(0, 2)
     own(3)
+    forward(2, 1)
+    forward(1, 2)
+    forward(0, 3)
+    forward(3, 1)
+    w_copy.wait_recv()
+    w_share.start()
+    forward(2, 2)
+    forward(1, 3)
     forward(0, 4)
+    forward(3, 2)
+    w_share.wait_recv()
+    project(0)
+    forward(2, 3)
     forward(1, 4)
-    w_copy.wait()
-    project(0)
-    for n in (1, 2, 3, 4):
-        forward(2, n)
-        forward(3, n)
+    forward(3, 3)
     project(1)
-    collect(0)
-    collect(1)
+    forward(2, 4)
+    project(2)
+    forward(3, 4)
+    project(3)
+    for j in range(4):
+        collect(j)
 
     for zz in range(Z):
 
@@ -280,6 +318,8 @@
 
     for copy in mate:
         copy.wait_send()
+    w_copy.wait_send()
+    w_share.wait_send()
     for j in range(4):
         for n in range(1, 5):
             if up_has(j, n):
@@ -288,12 +328,13 @@
                 down(j, n).wait_send()
     for _, copy in sent:
         copy.wait_send()
-    for t in range(2):
-        for q in range(4):
-
-            @pl.when(z != 2 * q + t)
+    for j in range(4):
+        for q in range(2):
+            owner, copy = to_plane(j, q)
+
+            @pl.when(z != owner)
             def _():
-                remote(sum_ref.at[t, q], plane_ref.at[z], z_s.at[t, q], z_r.at[z], 2 * (2 * q + t) + half, k).wait_send()
+                copy.wait_send()
 
     for zz in range(Z):
 
@@ -304,12 +345,13 @@
 
 def local(features, lengths, ids, taps, filters, skip, out_weight, embedding):
     vmem = pl.BlockSpec(memory_space=pltpu.VMEM)
+    hbm = pl.BlockSpec(memory_space=pl.ANY)
     dma = pltpu.SemaphoreType.DMA
     tile = (B, B)
     return pl.pallas_call(
         kernel,
         out_shape=jax.ShapeDtypeStruct((B, CHAN * B), BF16),
-        in_specs=[pl.BlockSpec(memory_space=pltpu.SMEM)] + [vmem] * 7,
+        in_specs=[pl.BlockSpec(memory_space=pltpu.SMEM), vmem, vmem, vmem, vmem, hbm, vmem, hbm],
         out_specs=vmem,
         scratch_shapes=[
             pltpu.VMEM((16, CHAN * B), BF16),
@@ -320,20 +362,23 @@
             pltpu.VMEM(((LAGS + SEQ) * PITCH, B), F32),
             pltpu.VMEM((SEQ * PITCH, B), F32),
             pltpu.VMEM((2, 8, OWN, B), BF16),
-            pltpu.VMEM((8, B, CHAN * B), BF16),
-            pltpu.VMEM((8, Z, 2, OWN, B), BF16),
-            pltpu.VMEM((2, CHAN, 4) + tile, BF16),
-            pltpu.VMEM((2, CHAN, 4) + tile, BF16),
-            pltpu.VMEM((2, 4) + tile, BF16),
+            pltpu.VMEM((8, 2, OWN, B), BF16),
+            pltpu.VMEM((CHAN, CHAN * B, B), BF16),
+            pltpu.VMEM(embedding.shape, BF16),
+            pltpu.VMEM((8, Z) + tile, BF16),
+            pltpu.VMEM((4, CHAN, 2) + tile, BF16),
+            pltpu.VMEM((4, CHAN, 2) + tile, BF16),
+            pltpu.VMEM((4, 2) + tile, BF16),
             pltpu.VMEM((Z,) + tile, BF16),
             pltpu.VMEM((CHAN,) + tile, BF16),
             pltpu.VMEM((B, CHAN * B), BF16),
-            dma, dma, dma, dma,
-            dma((SEQ,)), dma((SEQ,)),
+            dma((4,)), dma,
+            dma, dma, dma, dma, dma, dma,
+            dma((SEQ,)), dma((SEQ,)), dma((SEQ,)), dma((SEQ,)),
             dma((4,)), dma((4,)),
             dma((4, 5)), dma((4, 5)), dma((4, 5)), dma((4, 5)),
-            dma((2, CHAN)), dma((2, CHAN)),
-            dma((2, 4)), dma((Z,)),
+            dma((4, CHAN)), dma((4, CHAN)),
+            dma((4, 2)), dma((Z,)),
             dma((Z,)), dma((CHAN,)),
         ],
         compiler_params=pltpu.CompilerParams(

time: 107 us -> 89.7 us (0.84); the launches traced: 105 us -> 89.6 us
  Pallas kernels: 103 us -> 87.9 us
    pallas_call x1, Pallas kernels: 103 us -> 87.9 us  [local(): pl.pallas_call(kernel, out_shape=jax.ShapeDtypeStruct((B, CHAN * B), BF16...]
where the time goes in v1:
time: 89.7 us; the launch traced here: 89.6 us
  Pallas kernels  87.9 us (98%)
  local copies, waits for them, and re-layouts  1.67 us (2%)
    pallas_call x1, Pallas kernels, local(): pl.pallas_call(kernel, out_shape=jax.ShapeDtypeStruct((B, CHAN * B), BF16...  87.9 us

profile of v1, /device:TPU:104, one launch (start us, length us, event | category | flops | bytes accessed | tf_op | source)
XLA Modules:
  0.0 89.6 jit_solution(17483252909476661020)
XLA Ops:
  0.0 87.9 %hyena_block.1 = bf16[128,1024]{1,0:T(8,128)(2,1)} custom-call(s32[3]{0:T(128)} %len_ref.1, bf16[3,128,1024]{2,1,0:T(8,128)(2,1)} %bitcast.3, f32[3,3,1024]{2,1,0:T(4,128)} %taps_ref.1, f32[64,2048]{1,0:T(8,128)} %filt_ref.1, f32[1,64]{1,0:T(1,128)} %bitcast.4, bf16[1024,512]{1,0:T(8,128)(2,1)} %w_hbm.1, s32[1,128]{1,0:T(1,128)} %bitcast.5, ...), custom_call_target="tpu_custom_call" | custom-call | tf_op jit(solution)/shard_map/hyena_block/pallas_call | solution.py:351
  87.9 1.7 %copy.10 = bf16[128,1024]{1,0:T(8,128)(2,1)} copy(bf16[128,1024]{1,0:T(8,128)(2,1)} %hyena_block.1) | data formatting | bytes 524288

commit v2 on v1

--- a/solution.py
+++ b/solution.py
@@ -40,29 +40,25 @@
     return (position >= b1).astype(jnp.int32) + (position >= b2).astype(jnp.int32)
 
 
-def short_convolve(feat_ref, taps_ref, halo_ref, cols_ref, s, b1, b2):
+def short_agreement(s, b1, b2):
     row = lax.broadcasted_iota(jnp.int32, (B, B), 0)
     position = s * B + row
     here = document(position, b1, b2)
     agree1 = ((document(position - 1, b1, b2) == here) & (position >= 1)).astype(F32)
     agree2 = ((document(position - 2, b1, b2) == here) & (position >= 2)).astype(F32)
-    for n in range(8):
-        cols = slice(n * B, (n + 1) * B)
-        halo = halo_ref[:, cols].astype(F32)
-        short = []
-        for g in range(3):
-            x = feat_ref[g, :, cols].astype(F32)
-            older, newer = halo[2 * g : 2 * g + 1], halo[2 * g + 1 : 2 * g + 2]
-            x1 = jnp.where(row < 1, newer, pltpu.roll(x, 1, 0))
-            x2 = jnp.where(row < 1, older, jnp.where(row < 2, newer, pltpu.roll(x, 2, 0)))
-            t = taps_ref[:, g, cols]
-            running = t[0:1] * x + t[1:2] * x1 * agree1 + t[2:3] * x2 * agree2
-            short.append(running.astype(BF16))
-        product = (short[1].astype(F32) * short[2].astype(F32)).astype(BF16).T
-        query = short[0].T
-        for h in range(2):
-            cols_ref[2 * n + h, 0:OWN, :] = product[h * OWN : (h + 1) * OWN]
-            cols_ref[2 * n + h, OWN:B, :] = query[h * OWN : (h + 1) * OWN]
+    return row, agree1, agree2
+
+
+def short_convolve(feat_ref, taps_ref, halo_ref, agreement, g, n):
+    row, agree1, agree2 = agreement
+    cols = pl.ds(pl.multiple_of(n * B, B), B)
+    x = feat_ref[g, :, cols].astype(F32)
+    halo = halo_ref[:, cols].astype(F32)
+    older, newer = halo[2 * g : 2 * g + 1], halo[2 * g + 1 : 2 * g + 2]
+    x1 = jnp.where(row < 1, newer, pltpu.roll(x, 1, 0))
+    x2 = jnp.where(row < 1, older, jnp.where(row < 2, newer, pltpu.roll(x, 2, 0)))
+    t = [taps_ref[lag, pl.ds(g, 1), cols] for lag in range(3)]
+    return (t[0] * x + t[1] * x1 * agree1 + t[2] * x2 * agree2).astype(BF16)
 
 
 def long_convolve(toep_ref, x_ref, y_ref, b1, b2):
@@ -92,9 +88,9 @@
 def kernel(
     len_ref, feat_ref, taps_ref, filt_ref, skip_ref, w_hbm, ids_ref, emb_hbm, out_ref,
     halo_out, halo_in, cols_ref, rows_ref, toep_ref, x_ref, y_ref, gated_ref, pair_ref, w_ref, emb_ref, g_ref,
-    part_ref, got_ref, sum_ref, plane_ref, last_ref, look_ref,
+    part_y, part_x, got_y, got_x, mid_y, mid_x, end_y, end_x, sum_ref, plane_ref, last_ref, look_ref,
     own_s, emb_s, halo_s, halo_r, w_s, w_r, sib_s, sib_r, p_s, p_r, q_s, q_r, y_s, y_r,
-    up_s, up_r, down_s, down_r, rs_s, rs_r, z_s, z_r, f_s, f_r,
+    up_s, up_r, down_s, down_r, ya_s, ya_r, yb_s, yb_r, xa_s, xa_r, xb_s, xb_r, z_s, z_r, f_s, f_r,
 ):
     dp = lax.axis_index("dp")
     s = lax.axis_index("seq")
@@ -131,17 +127,45 @@
 
     halo_copy = remote(halo_out, halo_in, halo_s, halo_r, (s + 1) % SEQ, k)
     halo_copy.start()
+    for copy in own_w:
+        copy.wait()
+    depth = w_ref.shape[1] // 2
+    mine = w_ref.at[pl.ds(half * 4, 4), pl.ds(dp * depth, depth)]
+    w_copy = remote(mine, mine, w_s, w_r, mate_seq, k)
+    theirs = w_ref.at[pl.ds((1 - half) * 4, 4), pl.ds(dp * depth, depth)]
+    w_share = remote(theirs, theirs, sib_s, sib_r, s, k, 1 - dp)
     build_toeplitz(filt_ref, toep_ref, 0, 2)
     halo_copy.wait()
-    short_convolve(feat_ref, taps_ref, halo_in, cols_ref, s, b1, b2)
-
-    spread = []
-    for rows, send, recv in ((pl.ds(0, OWN), p_s, p_r), (pl.ds(OWN, OWN), q_s, q_r)):
-        for d in range(1, SEQ):
-            to = (s + d) % SEQ
-            copy = remote(cols_ref.at[to, rows], rows_ref.at[s, rows], send.at[d], recv.at[d], to, k)
-            copy.start()
-            spread.append(copy)
+    agreement = short_agreement(s, b1, b2)
+
+    def spread(n, e, rows, send, recv):
+        to = (z + n) % Z * 2 + (half if e == 0 else 1 - half)
+        return remote(cols_ref.at[to, rows], rows_ref.at[s, rows], send.at[n, e], recv.at[n, e], to, k)
+
+    first_rows, last_rows = pl.ds(0, OWN), pl.ds(OWN, OWN)
+    products, queries = [], []
+    order = (4, 3, 5, 2, 6, 1, 7, 0)
+    for n in order:
+        there = (z + n) % Z
+        short = [
+            short_convolve(feat_ref, taps_ref, halo_in, agreement, g, there).astype(F32) for g in (1, 2)
+        ]
+        product = (short[0] * short[1]).astype(BF16).T
+        for h in range(2):
+            cols_ref[2 * there + h, 0:OWN, :] = product[h * OWN : (h + 1) * OWN]
+        for e in range(2):
+            if n or e:
+                products.append(spread(n, e, first_rows, p_s, p_r))
+                products[-1].start()
+    for n in order:
+        there = (z + n) % Z
+        query = short_convolve(feat_ref, taps_ref, halo_in, agreement, 0, there).T
+        for h in range(2):
+            cols_ref[2 * there + h, OWN:B, :] = query[h * OWN : (h + 1) * OWN]
+        for e in range(2):
+            if n or e:
+                queries.append(spread(n, e, last_rows, q_s, q_r))
+                queries[-1].start()
     rows_ref[s] = cols_ref[s]
     build_toeplitz(filt_ref, toep_ref, 2, 8)
 
@@ -155,103 +179,129 @@
         look_ref[:, cols] = jnp.dot(hot, emb_ref[:, cols], preferred_element_type=F32).astype(BF16)
     skip = jnp.broadcast_to(skip_ref[...], (B, OWN)).T
 
-    for copy in spread[: SEQ - 1]:
+    for copy in products:
         copy.wait()
     x_ref[0 : LAGS * PITCH, :] = jnp.zeros((LAGS * PITCH, B), F32)
     for i in range(SEQ):
         at = (LAGS + i) * PITCH
         x_ref[at : at + OWN, :] = rows_ref[i, 0:OWN, :].astype(F32)
     long_convolve(toep_ref, x_ref, y_ref, b1, b2)
-    for copy in spread[SEQ - 1 :]:
+    for copy in queries:
         copy.wait()
-    for i in range(SEQ):
-        signal = rows_ref[i, 0:OWN, :].astype(F32)
-        convolved = (y_ref[i * PITCH : i * PITCH + OWN, :] + skip * signal).astype(BF16)
-        gated = rows_ref[i, OWN:B, :].astype(F32) * convolved.astype(F32)
-        owner = i // 2
-        gated_ref[i % 2, 2 * (owner % 4) + owner // 4] = gated.astype(BF16)
-
     mate = []
-    for j in range(4):
-        two = pl.ds(2 * j, 2)
-        copy = remote(gated_ref.at[1 - half, two], pair_ref.at[two, half], y_s.at[j], y_r.at[j], mate_seq, k)
+    for c in range(Z):
+        for parity in range(2):
+            i = 2 * (c // 2 + 4 * (c % 2)) + parity
+            signal = rows_ref[i, 0:OWN, :].astype(F32)
+            convolved = (y_ref[i * PITCH : i * PITCH + OWN, :] + skip * signal).astype(BF16)
+            gated = rows_ref[i, OWN:B, :].astype(F32) * convolved.astype(F32)
+            gated_ref[parity, c] = gated.astype(BF16)
+        copy = remote(gated_ref.at[1 - half, c], pair_ref.at[c, half], y_s.at[c], y_r.at[c], mate_seq, k)
         copy.start()
         mate.append(copy)
-    for copy in own_w:
-        copy.wait()
-    depth = w_ref.shape[1] // 2
-    mine = w_ref.at[pl.ds(half * 4, 4), pl.ds(dp * depth, depth)]
-    w_copy = remote(mine, mine, w_s, w_r, mate_seq, k)
+    for c in range(Z):
+        pair_ref[c, half] = gated_ref[half, c]
+
     w_copy.start()
-    theirs = w_ref.at[pl.ds((1 - half) * 4, 4), pl.ds(dp * depth, depth)]
-    w_share = remote(theirs, theirs, sib_s, sib_r, s, k, 1 - dp)
-    for q in range(8):
-        pair_ref[q, half] = gated_ref[half, q]
-
     up_seq, down_seq = (z + 1) % Z * 2 + half, (z + Z - 1) % Z * 2 + half
 
-    def up(j, n):
-        block = g_ref.at[pl.ds(2 * j, 2), (z + Z - n + 1) % Z]
-        return remote(block, block, up_s.at[j, n], up_r.at[j, n], up_seq, k)
-
-    def down(j, n):
-        block = g_ref.at[pl.ds(2 * j, 2), (z + n - 1) % Z]
-        return remote(block, block, down_s.at[j, n], down_r.at[j, n], down_seq, k)
-
-    def up_has(j, n):
-        return n <= 3 + (j % 2 == 0)
-
-    def down_has(j, n):
-        return n <= 3 + (j % 2 == 1)
-
-    def own(j):
-        mate[j].wait_recv()
-        for q in (2 * j, 2 * j + 1):
-            g_ref[q, z] = pair_ref[q].reshape(B, B).T
-        up(j, 1).start()
-        down(j, 1).start()
-
-    def forward(j, n):
-        if up_has(j, n):
-            up(j, n).wait_recv()
-            if up_has(j, n + 1):
-                up(j, n + 1).start()
-        if down_has(j, n):
-            down(j, n).wait_recv()
-            if down_has(j, n + 1):
-                down(j, n + 1).start()
-
-    sent = []
-
-    def project(j):
+    def up(c, n):
+        block = g_ref.at[c, (z + Z - n + 1) % Z]
+        return remote(block, block, up_s.at[c, n], up_r.at[c, n], up_seq, k)
+
+    def down(c, n):
+        block = g_ref.at[c, (z + n - 1) % Z]
+        return remote(block, block, down_s.at[c, n], down_r.at[c, n], down_seq, k)
+
+    def up_has(c, n):
+        return n <= 3 + (c % 2 == 0)
+
+    def down_has(c, n):
+        return n <= 3 + (c % 2 == 1)
+
+    def own(c):
+        mate[c].wait_recv()
+        g_ref[c, z] = pair_ref[c].reshape(B, B).T
+        up(c, 1).start()
+        down(c, 1).start()
+
+    def forward(c, n):
+        if up_has(c, n):
+            up(c, n).wait_recv()
+            if up_has(c, n + 1):
+                up(c, n + 1).start()
+        if down_has(c, n):
+            down(c, n).wait_recv()
+            if down_has(c, n + 1):
+                down(c, n + 1).start()
+
+    yl, x = k // 4, k % 4
+    across = (1 - yl) * 4 + x
+
+    def along(e):
+        return yl * 4 + (x + e) % 4
+
+    def first_y(j):
+        return remote(part_y.at[j, pl.ds((1 - yl) * 4, 4)], got_y.at[j], ya_s.at[j], ya_r.at[j], s, across)
+
+    def second_x(j, e):
+        return remote(mid_y.at[j, e], end_y.at[j, e], yb_s.at[j, e], yb_r.at[j, e], s, along(e))
+
+    def first_x(j, e):
+        return remote(
+            part_x.at[j, pl.ds((x + e) % 4 * 2, 2)], got_x.at[j, e], xa_s.at[j, e], xa_r.at[j, e], s, along(e)
+        )
+
+    def second_y(j):
+        return remote(mid_x.at[j, 1 - yl], end_x.at[j], xb_s.at[j], xb_r.at[j], s, across)
+
+    def project(j, turns):
         lhs = jnp.concatenate(
             [jnp.concatenate([g_ref[q, zz] for zz in range(Z)], axis=1) for q in (2 * j, 2 * j + 1)], axis=0
         )
-        for pair in ((1, 7), (2, 6), (3, 5), (4, 0)):
-            rhs = jnp.concatenate([w_ref[(k + d) % CHAN] for d in pair], axis=1)
+        for e in turns:
+            there = (x + e) % 4
+            rhs = jnp.concatenate([w_ref[there], w_ref[4 + there]], axis=1)
             value = jnp.dot(lhs, rhs, preferred_element_type=F32).astype(BF16)
-            for n, d in enumerate(pair):
-                for q in range(2):
-                    part_ref[j, d, q] = value[q * B : (q + 1) * B, n * B : (n + 1) * B]
-                if d:
-                    copy = remote(
-                        part_ref.at[j, d], got_ref.at[j, d], rs_s.at[j, d], rs_r.at[j, d], s, (k + d) % CHAN
-                    )
-                    copy.start()
-                    sent.append((j, copy))
+            for n in range(2):
+                part_y[j, n * 4 + there] = value[0:B, n * B : (n + 1) * B]
+                part_x[j, there * 2 + n] = value[B : 2 * B, n * B : (n + 1) * B]
+            if e:
+                first_x(j, e).start()
+            else:
+                first_y(j).start()
+
+    def middle(j):
+        first_y(j).wait_recv()
+        for e in (2, 1, 3, 0):
+            there = (x + e) % 4
+            total = part_y[j, yl * 4 + there].astype(F32) + got_y[j, there].astype(F32)
+            mid_y[j, e] = total.astype(BF16)
+            if e:
+                second_x(j, e).start()
+        for e in (1, 2, 3):
+            first_x(j, e).wait_recv()
+        for n in range(2):
+            total = part_x[j, x * 2 + n].astype(F32)
+            for e in (1, 2, 3):
+                total = total + got_x[j, e, n].astype(F32)
+            mid_x[j, n] = total.astype(BF16)
+        second_y(j).start()
 
     def to_plane(j, q):
         owner = j + 4 * q
         return owner, remote(sum_ref.at[j, q], plane_ref.at[z], z_s.at[j, q], z_r.at[z], owner * 2 + half, k)
 
     def collect(j):
-        for u, copy in sent:
-            if u == j:
-                copy.wait_recv()
         for q in range(2):
-            total = part_ref[j, 0, q].astype(F32)
-            for d in range(1, CHAN):
-                total = total + got_ref[j, d, q].astype(F32)
+            if q == 0:
+                total = mid_y[j, 0].astype(F32)
+                for e in (1, 2, 3):
+                    second_x(j, e).wait_recv()
+                    total = total + end_y[j, e].astype(F32)
+            else:
+                second_y(j).wait_recv()
+                total = mid_x[j, yl].astype(F32) + end_x[j].astype(F32)
             sum_ref[j, q] = total.astype(BF16)
             owner, copy = to_plane(j, q)
 
@@ -265,34 +315,63 @@
 
     own(0)
     own(1)
+    own(2)
+    own(3)
+    own(4)
+    own(5)
+    own(6)
+    own(7)
     forward(0, 1)
-    own(2)
     forward(1, 1)
+    forward(2, 1)
+    forward(3, 1)
+    forward(4, 1)
+    forward(5, 1)
+    forward(6, 1)
+    forward(7, 1)
     forward(0, 2)
-    own(3)
-    forward(2, 1)
     forward(1, 2)
-    forward(0, 3)
-    forward(3, 1)
+    forward(2, 2)
+    forward(3, 2)
+    forward(4, 2)
+    forward(5, 2)
+    forward(6, 2)
+    forward(7, 2)
     w_copy.wait_recv()
     w_share.start()
-    forward(2, 2)
+    forward(0, 3)
     forward(1, 3)
+    forward(2, 3)
+    forward(3, 3)
+    forward(4, 3)
+    forward(5, 3)
+    forward(6, 3)
+    forward(7, 3)
     forward(0, 4)
-    forward(3, 2)
+    forward(1, 4)
     w_share.wait_recv()
-    project(0)
-    forward(2, 3)
-    forward(1, 4)
-    forward(3, 3)
-    project(1)
+    project(0, (2, 1))
     forward(2, 4)
-    project(2)
     forward(3, 4)
-    project(3)
-    for j in range(4):
-        collect(j)
-
+    project(0, (3, 0))
+    forward(4, 4)
+    forward(5, 4)
+    project(1, (2, 1))
+    forward(6, 4)
+    forward(7, 4)
+    project(1, (3, 0))
+    project(2, (2, 1))
+    project(2, (3, 0))
+    project(3, (2, 1))
+    project(3, (3, 0))
+    middle(0)
+    middle(1)
+    middle(2)
+    middle(3)
+    collect(0)
+    collect(1)
+    collect(2)
+    collect(3)
     for zz in range(Z):
 
         @pl.when(z != zz)
@@ -320,14 +399,18 @@
         copy.wait_send()
     w_copy.wait_send()
     w_share.wait_send()
+    for c in range(Z):
+        for n in range(1, 5):
+            if up_has(c, n):
+                up(c, n).wait_send()
+            if down_has(c, n):
+                down(c, n).wait_send()
     for j in range(4):
-        for n in range(1, 5):
-            if up_has(j, n):
-                up(j, n).wait_send()
-            if down_has(j, n):
-                down(j, n).wait_send()
-    for _, copy in sent:
-        copy.wait_send()
+        first_y(j).wait_send()
+        second_y(j).wait_send()
+        for e in (1, 2, 3):
+            first_x(j, e).wait_send()
+            second_x(j, e).wait_send()
     for j in range(4):
         for q in range(2):
             owner, copy = to_plane(j, q)
@@ -366,18 +449,24 @@
             pltpu.VMEM((CHAN, CHAN * B, B), BF16),
             pltpu.VMEM(embedding.shape, BF16),
             pltpu.VMEM((8, Z) + tile, BF16),
-            pltpu.VMEM((4, CHAN, 2) + tile, BF16),
-            pltpu.VMEM((4, CHAN, 2) + tile, BF16),
+            pltpu.VMEM((4, CHAN) + tile, BF16),
+            pltpu.VMEM((4, CHAN) + tile, BF16),
+            pltpu.VMEM((4, 4) + tile, BF16),
+            pltpu.VMEM((4, 4, 2) + tile, BF16),
+            pltpu.VMEM((4, 4) + tile, BF16),
+            pltpu.VMEM((4, 2) + tile, BF16),
+            pltpu.VMEM((4, 4) + tile, BF16),
+            pltpu.VMEM((4,) + tile, BF16),
             pltpu.VMEM((4, 2) + tile, BF16),
             pltpu.VMEM((Z,) + tile, BF16),
             pltpu.VMEM((CHAN,) + tile, BF16),
             pltpu.VMEM((B, CHAN * B), BF16),
             dma((4,)), dma,
             dma, dma, dma, dma, dma, dma,
-            dma((SEQ,)), dma((SEQ,)), dma((SEQ,)), dma((SEQ,)),
-            dma((4,)), dma((4,)),
-            dma((4, 5)), dma((4, 5)), dma((4, 5)), dma((4, 5)),
-            dma((4, CHAN)), dma((4, CHAN)),
+            dma((Z, 2)), dma((Z, 2)), dma((Z, 2)), dma((Z, 2)),
+            dma((Z,)), dma((Z,)),
+            dma((Z, 5)), dma((Z, 5)), dma((Z, 5)), dma((Z, 5)),
+            dma((4,)), dma((4,)), dma((4, 4)), dma((4, 4)), dma((4, 4)), dma((4, 4)), dma((4,)), dma((4,)),
             dma((4, 2)), dma((Z,)),
             dma((Z,)), dma((CHAN,)),
         ],

time: 89.7 us -> 82.9 us (0.924)
  Pallas kernels: 87.9 us -> 80.8 us
    pallas_call x1, Pallas kernels: 87.9 us -> 80.8 us  [local(): pl.pallas_call(kernel, out_shape=jax.ShapeDtypeStruct((B, CHAN * B), BF16...]
where the time goes in v2:
time: 82.9 us; the launch traced here: 82.4 us
  Pallas kernels  80.8 us (97%)
  local copies, waits for them, and re-layouts  1.67 us (2%)
    pallas_call x1, Pallas kernels, local(): pl.pallas_call(kernel, out_shape=jax.ShapeDtypeStruct((B, CHAN * B), BF16...  80.8 us
    unnamed x1, local copies, waits for them, and re-layouts  1.67 us

profile of v2, /device:TPU:104, one launch (start us, length us, event | category | flops | bytes accessed | tf_op | source)
XLA Modules:
  0.0 82.4 jit_solution(7160486197260293955)
XLA Ops:
  0.0 80.8 %hyena_block.1 = bf16[128,1024]{1,0:T(8,128)(2,1)} custom-call(s32[3]{0:T(128)} %len_ref.1, bf16[3,128,1024]{2,1,0:T(8,128)(2,1)} %bitcast.3, f32[3,3,1024]{2,1,0:T(4,128)} %taps_ref.1, f32[64,2048]{1,0:T(8,128)} %filt_ref.1, f32[1,64]{1,0:T(1,128)} %bitcast.4, bf16[1024,512]{1,0:T(8,128)(2,1)} %w_hbm.1, s32[1,128]{1,0:T(1,128)} %bitcast.5, ...), custom_call_target="tpu_custom_call" | custom-call | tf_op jit(solution)/shard_map/hyena_block/pallas_call | solution.py:434
  80.8 1.7 %copy.10 = bf16[128,1024]{1,0:T(8,128)(2,1)} copy(bf16[128,1024]{1,0:T(8,128)(2,1)} %hyena_block.1) | data formatting | bytes 524288

commit v3 on v2

--- a/solution.py
+++ b/solution.py
@@ -86,10 +86,10 @@
 
 
 def kernel(
-    len_ref, feat_ref, taps_ref, filt_ref, skip_ref, w_hbm, ids_ref, emb_hbm, out_ref,
-    halo_out, halo_in, cols_ref, rows_ref, toep_ref, x_ref, y_ref, gated_ref, pair_ref, w_ref, emb_ref, g_ref,
+    len_ref, feat_hbm, taps_ref, filt_hbm, skip_ref, w_hbm, ids_ref, emb_hbm, out_ref,
+    feat_ref, filt_ref, halo_out, halo_in, cols_ref, rows_ref, toep_ref, x_ref, y_ref, gated_ref, pair_ref, w_ref, emb_ref, g_ref,
     part_y, part_x, got_y, got_x, mid_y, mid_x, end_y, end_x, sum_ref, plane_ref, last_ref, look_ref,
-    own_s, emb_s, halo_s, halo_r, w_s, w_r, sib_s, sib_r, p_s, p_r, q_s, q_r, y_s, y_r,
+    own_s, emb_s, feat_s, filt_s, halo_s, halo_r, w_s, w_r, sib_s, sib_r, p_s, p_r, q_s, q_r, y_s, y_r,
     up_s, up_r, down_s, down_r, ya_s, ya_r, yb_s, yb_r, xa_s, xa_r, xb_s, xb_r, z_s, z_r, f_s, f_r,
 ):
     dp = lax.axis_index("dp")
@@ -105,6 +105,10 @@
         pl.semaphore_signal(barrier, inc=1, device_id=(dp, s, (k + d) % CHAN), device_id_type=MESH)
     pl.semaphore_signal(barrier, inc=1, device_id=(1 - dp, s, k), device_id_type=MESH)
 
+    feat_copy = pltpu.make_async_copy(feat_hbm, feat_ref, feat_s)
+    filt_copy = pltpu.make_async_copy(filt_hbm.at[:, pl.ds(0, LAGS * B)], filt_ref, filt_s)
+    feat_copy.start()
+    filt_copy.start()
     own_w = [
         pltpu.make_async_copy(w_hbm.at[:, pl.ds(b * B, B)], w_ref.at[half * 4 + b], own_s.at[b]) for b in range(4)
     ]
@@ -121,19 +125,27 @@
             src_ref=src, dst_ref=dst, send_sem=send, recv_sem=recv, device_id=(core, seq, chan), device_id_type=MESH
         )
 
+    feat_copy.wait()
     edge = [feat_ref[g, B - 16 : B, :].astype(F32)[14:16] for g in range(3)]
     halo_out[...] = jnp.concatenate(edge + [jnp.zeros((10, CHAN * B), F32)], axis=0).astype(BF16)
     pl.semaphore_wait(barrier, SEQ - 1 + CHAN - 1 + 1)
 
     halo_copy = remote(halo_out, halo_in, halo_s, halo_r, (s + 1) % SEQ, k)
     halo_copy.start()
+    depth = w_ref.shape[1] // 2
+
+    def fetch(n):
+        mine = w_ref.at[pl.ds(half * 4 + 2 * n, 2), pl.ds(dp * depth, depth)]
+        return remote(mine, mine, w_s.at[n], w_r.at[n], mate_seq, k)
+
+    def share(n):
+        theirs = w_ref.at[pl.ds((1 - half) * 4 + 2 * n, 2), pl.ds(dp * depth, depth)]
+        return remote(theirs, theirs, sib_s.at[n], sib_r.at[n], s, k, 1 - dp)
+
     for copy in own_w:
         copy.wait()
-    depth = w_ref.shape[1] // 2
-    mine = w_ref.at[pl.ds(half * 4, 4), pl.ds(dp * depth, depth)]
-    w_copy = remote(mine, mine, w_s, w_r, mate_seq, k)
-    theirs = w_ref.at[pl.ds((1 - half) * 4, 4), pl.ds(dp * depth, depth)]
-    w_share = remote(theirs, theirs, sib_s, sib_r, s, k, 1 - dp)
+    fetch(0).start()
+    filt_copy.wait()
     build_toeplitz(filt_ref, toep_ref, 0, 2)
     halo_copy.wait()
     agreement = short_agreement(s, b1, b2)
@@ -202,15 +214,17 @@
     for c in range(Z):
         pair_ref[c, half] = gated_ref[half, c]
 
-    w_copy.start()
+    fetch(1).start()
+    fetch(0).wait_recv()
+    share(0).start()
     up_seq, down_seq = (z + 1) % Z * 2 + half, (z + Z - 1) % Z * 2 + half
 
     def up(c, n):
-        block = g_ref.at[c, (z + Z - n + 1) % Z]
+        block = g_ref.at[pl.ds(2 * c, 2), (z + Z - n + 1) % Z]
         return remote(block, block, up_s.at[c, n], up_r.at[c, n], up_seq, k)
 
     def down(c, n):
-        block = g_ref.at[c, (z + n - 1) % Z]
+        block = g_ref.at[pl.ds(2 * c, 2), (z + n - 1) % Z]
         return remote(block, block, down_s.at[c, n], down_r.at[c, n], down_seq, k)
 
     def up_has(c, n):
@@ -220,8 +234,9 @@
         return n <= 3 + (c % 2 == 1)
 
     def own(c):
-        mate[c].wait_recv()
-        g_ref[c, z] = pair_ref[c].reshape(B, B).T
+        for q in (2 * c, 2 * c + 1):
+            mate[q].wait_recv()
+            g_ref[q, z] = pair_ref[q].reshape(B, B).T
         up(c, 1).start()
         down(c, 1).start()
 
@@ -317,53 +332,30 @@
     own(1)
     own(2)
     own(3)
-    own(4)
-    own(5)
-    own(6)
-    own(7)
     forward(0, 1)
     forward(1, 1)
     forward(2, 1)
     forward(3, 1)
-    forward(4, 1)
-    forward(5, 1)
-    forward(6, 1)
-    forward(7, 1)
     forward(0, 2)
     forward(1, 2)
     forward(2, 2)
     forward(3, 2)
-    forward(4, 2)
-    forward(5, 2)
-    forward(6, 2)
-    forward(7, 2)
-    w_copy.wait_recv()
-    w_share.start()
+    fetch(1).wait_recv()
+    share(1).start()
     forward(0, 3)
     forward(1, 3)
     forward(2, 3)
     forward(3, 3)
-    forward(4, 3)
-    forward(5, 3)
-    forward(6, 3)
-    forward(7, 3)
     forward(0, 4)
+    share(0).wait_recv()
+    share(1).wait_recv()
+    project(0, (2, 1, 3, 0))
     forward(1, 4)
-    w_share.wait_recv()
-    project(0, (2, 1))
+    project(1, (2, 1, 3, 0))
     forward(2, 4)
+    project(2, (2, 1, 3, 0))
     forward(3, 4)
-    project(0, (3, 0))
-    forward(4, 4)
-    forward(5, 4)
-    project(1, (2, 1))
-    forward(6, 4)
-    forward(7, 4)
-    project(1, (3, 0))
-    project(2, (2, 1))
-    project(2, (3, 0))
-    project(3, (2, 1))
-    project(3, (3, 0))
+    project(3, (2, 1, 3, 0))
     middle(0)
     middle(1)
     middle(2)
@@ -372,6 +364,7 @@
     collect(1)
     collect(2)
     collect(3)
+
     for zz in range(Z):
 
         @pl.when(z != zz)
@@ -397,9 +390,10 @@
 
     for copy in mate:
         copy.wait_send()
-    w_copy.wait_send()
-    w_share.wait_send()
-    for c in range(Z):
+    for n in range(2):
+        fetch(n).wait_send()
+        share(n).wait_send()
+    for c in range(4):
         for n in range(1, 5):
             if up_has(c, n):
                 up(c, n).wait_send()
@@ -434,9 +428,11 @@
     return pl.pallas_call(
         kernel,
         out_shape=jax.ShapeDtypeStruct((B, CHAN * B), BF16),
-        in_specs=[pl.BlockSpec(memory_space=pltpu.SMEM), vmem, vmem, vmem, vmem, hbm, vmem, hbm],
+        in_specs=[pl.BlockSpec(memory_space=pltpu.SMEM), hbm, vmem, hbm, vmem, hbm, vmem, hbm],
         out_specs=vmem,
         scratch_shapes=[
+            pltpu.VMEM((3, B, CHAN * B), BF16),
+            pltpu.VMEM((OWN, LAGS * B), F32),
             pltpu.VMEM((16, CHAN * B), BF16),
             pltpu.VMEM((16, CHAN * B), BF16),
             pltpu.VMEM((SEQ,) + tile, BF16),
@@ -461,11 +457,11 @@
             pltpu.VMEM((Z,) + tile, BF16),
             pltpu.VMEM((CHAN,) + tile, BF16),
             pltpu.VMEM((B, CHAN * B), BF16),
-            dma((4,)), dma,
-            dma, dma, dma, dma, dma, dma,
+            dma((4,)), dma, dma, dma,
+            dma, dma, dma((2,)), dma((2,)), dma((2,)), dma((2,)),
             dma((Z, 2)), dma((Z, 2)), dma((Z, 2)), dma((Z, 2)),
             dma((Z,)), dma((Z,)),
-            dma((Z, 5)), dma((Z, 5)), dma((Z, 5)), dma((Z, 5)),
+            dma((4, 5)), dma((4, 5)), dma((4, 5)), dma((4, 5)),
             dma((4,)), dma((4,)), dma((4, 4)), dma((4, 4)), dma((4, 4)), dma((4, 4)), dma((4,)), dma((4,)),
             dma((4, 2)), dma((Z,)),
             dma((Z,)), dma((CHAN,)),

time: 82.9 us -> 82 us (0.989)
  no operation moved by 1% of the time
where the time goes in v3:
time: 82 us; the launch traced here: 81.8 us
  Pallas kernels  80.1 us (98%)
  local copies, waits for them, and re-layouts  1.67 us (2%)
    pallas_call x1, Pallas kernels, local(): pl.pallas_call(kernel, out_shape=jax.ShapeDtypeStruct((B, CHAN * B), BF16...  80.1 us
    unnamed x1, local copies, waits for them, and re-layouts  1.67 us

profile of v3, /device:TPU:104, one launch (start us, length us, event | category | flops | bytes accessed | tf_op | source)
XLA Modules:
  0.0 81.8 jit_solution(6443315729106108445)
XLA Ops:
  0.0 80.1 %hyena_block.1 = bf16[128,1024]{1,0:T(8,128)(2,1)} custom-call(s32[3]{0:T(128)} %len_ref.1, bf16[3,128,1024]{2,1,0:T(8,128)(2,1)} %bitcast.3, f32[3,3,1024]{2,1,0:T(4,128)} %taps_ref.1, f32[64,2048]{1,0:T(8,128)} %filt_hbm.1, f32[1,64]{1,0:T(1,128)} %bitcast.4, bf16[1024,512]{1,0:T(8,128)(2,1)} %w_hbm.1, s32[1,128]{1,0:T(1,128)} %bitcast.5, ...), custom_call_target="tpu_custom_call" | custom-call | tf_op jit(solution)/shard_map/hyena_block/pallas_call | solution.py:428
  80.1 1.7 %copy.10 = bf16[128,1024]{1,0:T(8,128)(2,1)} copy(bf16[128,1024]{1,0:T(8,128)(2,1)} %hyena_block.1) | data formatting | bytes 524288

commit v4 on v3

--- a/solution.py
+++ b/solution.py
@@ -438,8 +438,8 @@
             pltpu.VMEM((SEQ,) + tile, BF16),
             pltpu.VMEM((SEQ,) + tile, BF16),
             pltpu.VMEM((OWN, (LAGS + 1) * B, B), BF16),
-            pltpu.VMEM(((LAGS + SEQ) * PITCH, B), F32),
-            pltpu.VMEM((SEQ * PITCH, B), F32),
+            pltpu.VMEM(((LAGS + SEQ + 1) * PITCH, B), F32),
+            pltpu.VMEM(((SEQ + 1) * PITCH, B), F32),
             pltpu.VMEM((2, 8, OWN, B), BF16),
             pltpu.VMEM((8, 2, OWN, B), BF16),
             pltpu.VMEM((CHAN, CHAN * B, B), BF16),

time: 82 us -> 82 us (level)
  no operation moved by 1% of the time
where the time goes in v4:
time: 82 us; the launch traced here: 81.8 us
  Pallas kernels  80.1 us (98%)
  local copies, waits for them, and re-layouts  1.67 us (2%)
    pallas_call x1, Pallas kernels, local(): pl.pallas_call(kernel, out_shape=jax.ShapeDtypeStruct((B, CHAN * B), BF16...  80.1 us
    unnamed x1, local copies, waits for them, and re-layouts  1.67 us

profile of v4, /device:TPU:104, one launch (start us, length us, event | category | flops | bytes accessed | tf_op | source)
XLA Modules:
  0.0 81.8 jit_solution(13216173130579817046)
XLA Ops:
  0.0 80.1 %hyena_block.1 = bf16[128,1024]{1,0:T(8,128)(2,1)} custom-call(s32[3]{0:T(128)} %len_ref.1, bf16[3,128,1024]{2,1,0:T(8,128)(2,1)} %bitcast.3, f32[3,3,1024]{2,1,0:T(4,128)} %taps_ref.1, f32[64,2048]{1,0:T(8,128)} %filt_hbm.1, f32[1,64]{1,0:T(1,128)} %bitcast.4, bf16[1024,512]{1,0:T(8,128)(2,1)} %w_hbm.1, s32[1,128]{1,0:T(1,128)} %bitcast.5, ...), custom_call_target="tpu_custom_call" | custom-call | tf_op jit(solution)/shard_map/hyena_block/pallas_call | solution.py:428
  80.1 1.7 %copy.10 = bf16[128,1024]{1,0:T(8,128)(2,1)} copy(bf16[128,1024]{1,0:T(8,128)(2,1)} %hyena_block.1) | data formatting | bytes 524288

commit v5 on v4

--- a/solution.py
+++ b/solution.py
@@ -214,9 +214,6 @@
     for c in range(Z):
         pair_ref[c, half] = gated_ref[half, c]
 
-    fetch(1).start()
-    fetch(0).wait_recv()
-    share(0).start()
     up_seq, down_seq = (z + 1) % Z * 2 + half, (z + Z - 1) % Z * 2 + half
 
     def up(c, n):
@@ -332,6 +329,9 @@
     own(1)
     own(2)
     own(3)
+    fetch(1).start()
+    fetch(0).wait_recv()
+    share(0).start()
     forward(0, 1)
     forward(1, 1)
     forward(2, 1)

time: 82 us -> 81.9 us (level)
  no operation moved by 1% of the time
where the time goes in v5:
time: 81.9 us; the launch traced here: 81.4 us
  Pallas kernels  79.7 us (97%)
  local copies, waits for them, and re-layouts  1.67 us (2%)
    pallas_call x1, Pallas kernels, local(): pl.pallas_call(kernel, out_shape=jax.ShapeDtypeStruct((B, CHAN * B), BF16...  79.7 us
    unnamed x1, local copies, waits for them, and re-layouts  1.67 us

profile of v5, /device:TPU:104, one launch (start us, length us, event | category | flops | bytes accessed | tf_op | source)
XLA Modules:
  0.0 81.4 jit_solution(1291796567163335866)
XLA Ops:
  0.0 79.7 %hyena_block.1 = bf16[128,1024]{1,0:T(8,128)(2,1)} custom-call(s32[3]{0:T(128)} %len_ref.1, bf16[3,128,1024]{2,1,0:T(8,128)(2,1)} %bitcast.3, f32[3,3,1024]{2,1,0:T(4,128)} %taps_ref.1, f32[64,2048]{1,0:T(8,128)} %filt_hbm.1, f32[1,64]{1,0:T(1,128)} %bitcast.4, bf16[1024,512]{1,0:T(8,128)(2,1)} %w_hbm.1, s32[1,128]{1,0:T(1,128)} %bitcast.5, ...), custom_call_target="tpu_custom_call" | custom-call | tf_op jit(solution)/shard_map/hyena_block/pallas_call | solution.py:428
  79.7 1.7 %copy.10 = bf16[128,1024]{1,0:T(8,128)(2,1)} copy(bf16[128,1024]{1,0:T(8,128)(2,1)} %hyena_block.1) | data formatting | bytes 524288
